TPU v7x, 32 devices: a whole 2x2x4 slice. The times are simulated.
32 devices in a mesh: groups: 2 (over x), tm: 16 (over z, y, core).
Axes of the slice: x: 2, y: 2, z: 4, core: 2. Of those that a mesh axis runs over, the one named last changes fastest.
Arguments:
- hyper: float32 [6], P('groups'), parts along dimension 0, may hold values from 0.5 to 0.9
- spatial_prec: float32 [768, 768], replicated, as said below
- part_lengths: int32 [32], P('groups'), parts along dimension 0, may hold values from 1 to 2, as said below
- reading_index: int32 [4, 32, 1024], P(None, ('groups', 'tm')), parts along dimension 1, may hold values from 0 to 767, as said below
- reading_value: float32 [4, 32, 1024], P(None, ('groups', 'tm')), parts along dimension 1, as said below
- reading_cov: float32 [16, 32, 1024], P(None, ('groups', 'tm')), parts along dimension 1, may hold values from -0.1875 to 0.1875
Outputs:
- sep_block: float32 [32, 768, 768], P(('groups', 'tm')), parts along dimension 0
- fill_block: float32 [32, 768, 768], P(('groups', 'tm')), parts along dimension 0
- sep_border: float32 [32, 16, 768], P(('groups', 'tm')), parts along dimension 0
- tip: float32 [32, 16], P('groups'), parts along dimension 0
There are 2 independent parts, one for each index of `groups`. A program takes and returns all parts, laid end to end along the dimension named above; an argument that names none is the same for every part. Nothing has to cross between parts.
Inputs may be any that keep to these rules, and one draw needn't show every extreme that they name: `reading_index`: row 0 is a reading's day, rows 1 to 3 the mesh nodes of its triangle's vertices. On every device, column block k (columns k * 64 to (k + 1) * 64 - 1) holds readings whose day lies in time partition k. `part_lengths`: partition k holds the days that follow those of partitions 0 to k - 1; exactly 8 partitions hold 2 days, the others 1. `reading_value`: row 0 is the linear predictor; rows 1 to 3 are positive barycentric weights summing to 1 for each reading. `spatial_prec`: A symmetric sparse mesh precision: each row has a few nonpositive neighbour entries, and a positive diagonal that exceeds the sum of magnitudes of its row's other entries.
All inputs are finite; a program needn't handle non-finite values.
Results may differ from a plain program's by a relative error of at most 0.0003.
Values sent between devices are 32-bit elements; how exact they have to be, the bound alone decides.
A program may use at most 128 MiB of HBM per device.

v0:
```python
import functools

import jax
import jax.numpy as jnp
from jax import lax
from jax.experimental import pallas as pl
from jax.experimental.pallas import tpu as pltpu
from jax.sharding import PartitionSpec as P

HIGHEST = lax.Precision.HIGHEST
BF = jnp.bfloat16
F32 = jnp.float32
PAD = 128
TILE = 128
ASSUMED = 0.3
CLOSE = 0.7
SMALL = 0.006 * 0.006


def nn(a, b):
    return lax.dot_general(a, b, (((1,), (0,)), ((), ())), preferred_element_type=F32)


def nt(a, b):
    return lax.dot_general(a, b, (((1,), (1,)), ((), ())), preferred_element_type=F32)


def nt3(ah, al, bh, bl):
    return nt(ah, bh) + nt(ah, bl) + nt(al, bh)


def split(x):
    hi = x.astype(BF)
    return hi, (x - hi.astype(F32)).astype(BF)


def eye_part(rows, cols, col_lo):
    r = lax.broadcasted_iota(jnp.int32, (rows, cols), 0)
    c = lax.broadcasted_iota(jnp.int32, (rows, cols), 1) + col_lo
    return jnp.where(r == c, 1.0, 0.0).astype(F32)


def next_bound(a):
    q = a * (2.0 - a)
    return 2.0 / (1.0 + q), 2.0 * q / (1.0 + q)


def partition_kernel(
    chunk, nblk, hyper_ref, meta_ref, prec_ref, recs_ref,
    sep_ref, fill_ref, packed_ref, border_ref, lateral_ref, tip_ref,
    sh, sl, h1, b1, ah, al, x, res, rth, rtl, yt, rest, wt, a32, x32, t32,
):
    m = prec_ref.shape[0]
    covars = border_ref.shape[0]
    rho, tau = hyper_ref[0], hyper_ref[1]
    c_diag = (1.0 + rho * rho) * tau
    c_off = -rho * tau
    my_end, length, position = meta_ref[0], meta_ref[1], meta_ref[2]
    end_f = my_end.astype(F32)
    two = length == 2

    sep_ref[...] = c_diag * prec_ref[...]
    h1[...] = c_diag * prec_ref[...]
    b1[...] = jnp.zeros_like(b1)
    border_ref[...] = jnp.zeros_like(border_ref)
    tip_ref[...] = jnp.zeros_like(tip_ref)

    def add_chunk(j, _):
        lanes = pl.ds(pl.multiple_of(j * chunk, chunk), chunk)
        slot = end_f - recs_ref[0:1, lanes]
        m0 = jnp.where(slot == 0.0, 1.0, 0.0)
        m1 = jnp.where(slot == 1.0, 1.0, 0.0)
        root = jnp.exp(0.5 * recs_ref[4:5, lanes])
        ids = [recs_ref[u : u + 1, lanes] for u in (1, 2, 3)]
        vals = [recs_ref[u : u + 1, lanes] * root for u in (5, 6, 7)]

        def build(i, _):
            rows = pl.ds(pl.multiple_of(i * 64, 64), 64)
            node = (lax.broadcasted_iota(jnp.int32, (64, chunk), 0) + i * 64).astype(F32)
            s = jnp.where(node == ids[0], vals[0], 0.0)
            s = s + jnp.where(node == ids[1], vals[1], 0.0)
            s = s + jnp.where(node == ids[2], vals[2], 0.0)
            hi, lo = split(s)
            sh[rows, :] = hi
            sl[rows, :] = lo
            return 0

        lax.fori_loop(0, m // 64, build, 0)
        z = recs_ref[8 : 8 + covars, lanes] * root
        z = jnp.concatenate([z, jnp.zeros((PAD - covars, chunk), F32)], axis=0)
        zh, zl = split(z)
        tip_ref[...] += nt3(zh, zl, zh, zl)[:covars, :covars]
        m0h = m0.astype(BF)
        m1h = m1.astype(BF)

        def grow(i, _):
            rows = pl.ds(pl.multiple_of(i * nblk, nblk), nblk)
            bh, bl = sh[rows, :], sl[rows, :]
            bh0, bl0, bh1, bl1 = bh * m0h, bl * m0h, bh * m1h, bl * m1h
            sep_ref[:, rows] += nt3(sh[...], sl[...], bh0, bl0)
            h1[:, rows] += nt3(sh[...], sl[...], bh1, bl1)
            border_ref[:, rows] += nt3(zh, zl, bh0, bl0)[:covars]
            b1[:, rows] += nt3(zh, zl, bh1, bl1)
            return 0

        lax.fori_loop(0, m // nblk, grow, 0)
        return 0

    lax.fori_loop(0, recs_ref.shape[1] // chunk, add_chunk, 0)

    picked = eye_part(m, m, 0) * h1[...]
    d_row = lax.rsqrt(jnp.sum(picked, axis=0, keepdims=True))
    d_col = lax.rsqrt(jnp.sum(picked, axis=1, keepdims=True))
    scaled = h1[...] * d_row * d_col
    a32[...] = scaled
    hi, lo = split(scaled)
    ah[...] = hi
    al[...] = lo
    top = jnp.max(jnp.sum(jnp.abs(scaled), axis=0, keepdims=True))
    hi, lo = split(c_off * prec_ref[...] * d_row)
    rth[0:m, :] = hi
    rtl[0:m, :] = lo
    hi, lo = split(b1[...] * d_row)
    rth[m : m + PAD, :] = hi
    rtl[m : m + PAD, :] = lo

    a0 = jnp.float32(ASSUMED)
    alpha = (2.0 - a0) / top
    s0, a1 = next_bound(a0)
    x[0] = (s0 * alpha * (2.0 * eye_part(m, m, 0) - alpha * scaled)).astype(BF)

    def newton(state):
        k, a, _, cur = state
        s, later = next_bound(a)

        def residual(i, total):
            cols = pl.ds(pl.multiple_of(i * nblk, nblk), nblk)
            r = eye_part(m, nblk, i * nblk) - nn(ah[...], x[cur, :, cols])
            res[:, cols] = r.astype(BF)
            return jnp.maximum(total, jnp.sum(jnp.abs(r), axis=0, keepdims=True))

        total = jnp.max(lax.fori_loop(0, m // nblk, residual, jnp.zeros((1, nblk), F32)))

        def improve(i, _):
            cols = pl.ds(pl.multiple_of(i * nblk, nblk), nblk)
            old = x[cur, :, cols].astype(F32)
            x[1 - cur, :, cols] = (s * (old + nn(x[cur], res[:, cols]))).astype(BF)
            return 0

        lax.fori_loop(0, m // nblk, improve, 0)
        return k + 1, later, total, 1 - cur

    _, _, total, cur = lax.while_loop(
        lambda st: jnp.logical_and(st[0] < 10, st[2] > CLOSE),
        newton,
        (jnp.int32(0), a1, jnp.float32(1e9), jnp.int32(0)),
    )

    def first(i, _):
        cols = pl.ds(pl.multiple_of(i * nblk, nblk), nblk)
        yt[:, cols] = nn(rth[...], x[cur, :, cols]).astype(BF)
        return 0

    def second(i, sums):
        cols = pl.ds(pl.multiple_of(i * nblk, nblk), nblk)
        right = rth[:, cols].astype(F32)
        r = right - nn(yt[...], ah[:, cols])
        r = r + (rtl[:, cols].astype(F32) - nn(yt[...], al[:, cols]))
        rest[:, cols] = r.astype(BF)
        left_sum, right_sum = sums
        return (
            left_sum + jnp.sum(r * r, axis=0, keepdims=True),
            right_sum + jnp.sum(right * right, axis=0, keepdims=True),
        )

    steps = m // nblk
    lax.fori_loop(0, steps, first, 0)
    zero = jnp.zeros((1, nblk), F32)
    left_sum, right_sum = lax.fori_loop(0, steps, second, (zero, zero))
    good = jnp.logical_and(total <= CLOSE, jnp.sum(left_sum) <= SMALL * jnp.sum(right_sum))

    def put_result(cols_lo, width, col):
        cols = pl.ds(cols_lo, width)
        u = jnp.where(two, -col[:m], 0.0)
        sep_ref[:, cols] += u
        fill_ref[:, cols] = jnp.where(
            position == 0, 0.0, jnp.where(two, u, c_off * prec_ref[:, cols])
        )
        side = jnp.where(two, -col[m : m + covars], 0.0)
        border_ref[:, cols] += side
        lateral_ref[:, cols] = side

    def put_tip(block):
        tip_ref[...] += jnp.where(two, -block[:covars, :covars], 0.0)

    @pl.when(good)
    def _():
        def third(i, _):
            cols = pl.ds(pl.multiple_of(i * nblk, nblk), nblk)
            w = yt[:, cols].astype(F32) + nn(rest[...], x[cur, :, cols])
            wt[:, cols] = w.astype(BF)
            return 0

        def last(i, _):
            lo = pl.multiple_of(i * nblk, nblk)
            rows = pl.ds(lo, nblk)
            col = nt(rth[...], yt[rows, :]) + nt(rtl[...], yt[rows, :]) + nt(wt[...], rest[rows, :])
            put_result(lo, nblk, col)
            return 0

        lax.fori_loop(0, steps, third, 0)
        lax.fori_loop(0, steps, last, 0)
        tail = pl.ds(m, PAD)
        put_tip(
            nt(rth[tail, :], yt[tail, :])
            + nt(rtl[tail, :], yt[tail, :])
            + nt(wt[tail, :], rest[tail, :])
        )

    @pl.when(jnp.logical_not(good))
    def _():
        blk = TILE
        bands = m // blk
        all_rows = m + PAD

        def exact(a, b):
            return lax.dot_general(
                a, b, (((1,), (0,)), ((), ())), precision=HIGHEST, preferred_element_type=F32
            )

        x32[0] = alpha * eye_part(m, m, 0)

        def step(state):
            k, a, _, cur = state
            s, later = next_bound(a)

            def residual(i, total):
                cols = pl.ds(pl.multiple_of(i * blk, blk), blk)
                r = eye_part(m, blk, i * blk) - exact(a32[...], x32[cur, :, cols])
                t32[0:m, cols] = r
                return total + jnp.sum(r * r)

            total = lax.fori_loop(0, bands, residual, jnp.float32(0.0))

            def improve(i, _):
                cols = pl.ds(pl.multiple_of(i * blk, blk), blk)
                x32[1 - cur, :, cols] = s * (
                    x32[cur, :, cols] + exact(x32[cur], t32[0:m, cols])
                )
                return 0

            lax.fori_loop(0, bands, improve, 0)
            return k + 1, later, total, 1 - cur

        _, _, _, cur32 = lax.while_loop(
            lambda st: jnp.logical_and(st[0] < 40, st[2] > 1e-3),
            step,
            (jnp.int32(0), a0, jnp.float32(1e9), jnp.int32(0)),
        )
        inv = x32.at[cur32]

        def right(lo):
            return rth[pl.ds(lo, blk), :].astype(F32) + rtl[pl.ds(lo, blk), :].astype(F32)

        def solve(i, _):
            lo = pl.multiple_of(i * blk, blk)
            r = right(lo)
            y = exact(r, inv[...])
            for _ in range(2):
                y = y + exact(r - exact(y, a32[...]), inv[...])
            t32[pl.ds(lo, blk), :] = y
            return 0

        lax.fori_loop(0, all_rows // blk, solve, 0)

        def exact_nt(a, b):
            return lax.dot_general(
                a, b, (((1,), (1,)), ((), ())), precision=HIGHEST, preferred_element_type=F32
            )

        whole = rth[...].astype(F32) + rtl[...].astype(F32)

        def last(i, _):
            lo = pl.multiple_of(i * blk, blk)
            put_result(lo, blk, exact_nt(whole, t32[pl.ds(lo, blk), :]))
            return 0

        lax.fori_loop(0, bands, last, 0)
        put_tip(exact_nt(right(m), t32[pl.ds(m, PAD), :]))

    at = 0
    for r in range(m // TILE):
        for c in range(r + 1):
            packed_ref[at * TILE : (at + 1) * TILE, :] = fill_ref[
                r * TILE : (r + 1) * TILE, c * TILE : (c + 1) * TILE
            ]
            at += 1


def add_kernel(meta_ref, own_ref, packed_ref, border_ref, side_ref, sep_ref, out_border_ref):
    m = own_ref.shape[0]
    take = meta_ref[3] == 2
    at = 0
    for r in range(m // TILE):
        for c in range(r + 1):
            block = jnp.where(take, packed_ref[at * TILE : (at + 1) * TILE, :], 0.0)
            rs, cs = slice(r * TILE, (r + 1) * TILE), slice(c * TILE, (c + 1) * TILE)
            sep_ref[rs, cs] = own_ref[rs, cs] + block
            if r != c:
                sep_ref[cs, rs] = own_ref[cs, rs] + block.T
            at += 1
    out_border_ref[...] = border_ref[...] + jnp.where(take, side_ref[...], 0.0)


def local(hyper, spatial_prec, part_lengths, reading_index, reading_value, reading_cov):
    m = spatial_prec.shape[0]
    covars = reading_cov.shape[0]
    tm = lax.axis_size("tm")
    reads = reading_index.shape[2]
    cap = reads // tm
    position = lax.axis_index("tm")
    fields = 8 + covars
    packed = jnp.concatenate(
        [reading_index[:, 0].astype(F32), reading_value[:, 0], reading_cov[:, 0]], axis=0
    )
    packed = packed.reshape(fields, tm, cap).transpose(1, 0, 2)
    packed = lax.all_to_all(packed, "tm", split_axis=0, concat_axis=0, tiled=True)
    recs = packed.transpose(1, 0, 2).reshape(fields, reads)

    upto = jnp.arange(tm, dtype=jnp.int32)
    my_end = jnp.sum(jnp.where(upto <= position, part_lengths, 0)) - 1
    my_len = jnp.sum(jnp.where(upto == position, part_lengths, 0))
    next_len = jnp.sum(jnp.where(upto == position + 1, part_lengths, 0))
    meta = jnp.stack([my_end, my_len, position, next_len]).astype(jnp.int32)

    chunk = min(reads, 1024)
    nblk = 256 if m % 256 == 0 else 128
    tiles = m // TILE
    packed_rows = tiles * (tiles + 1) // 2 * TILE
    vmem = pl.BlockSpec(memory_space=pltpu.VMEM)
    smem = pl.BlockSpec(memory_space=pltpu.SMEM)
    shape = lambda *s: jax.ShapeDtypeStruct(s, F32)
    own, fill, lower, border, lateral, tip = pl.pallas_call(
        functools.partial(partition_kernel, chunk, nblk),
        out_shape=(
            shape(m, m), shape(m, m), shape(packed_rows, TILE),
            shape(covars, m), shape(covars, m), shape(covars, covars),
        ),
        in_specs=[smem, smem, vmem, vmem],
        out_specs=[vmem] * 6,
        scratch_shapes=[
            pltpu.VMEM((m, chunk), BF),
            pltpu.VMEM((m, chunk), BF),
            pltpu.VMEM((m, m), F32),
            pltpu.VMEM((PAD, m), F32),
            pltpu.VMEM((m, m), BF),
            pltpu.VMEM((m, m), BF),
            pltpu.VMEM((2, m, m), BF),
            pltpu.VMEM((m, m), BF),
            pltpu.VMEM((m + PAD, m), BF),
            pltpu.VMEM((m + PAD, m), BF),
            pltpu.VMEM((m + PAD, m), BF),
            pltpu.VMEM((m + PAD, m), BF),
            pltpu.VMEM((m + PAD, m), BF),
            pltpu.VMEM((m, m), F32),
            pltpu.VMEM((2, m, m), F32),
            pltpu.VMEM((m + PAD, m), F32),
        ],
        compiler_params=pltpu.CompilerParams(vmem_limit_bytes=60 * 1024 * 1024),
        name="partition",
    )(hyper, meta, spatial_prec, recs)

    back = [(i + 1, i) for i in range(tm - 1)]
    from_right = lax.ppermute(lower, "tm", back)
    side_right = lax.ppermute(lateral, "tm", back)
    tip = lax.psum(tip, "tm") + hyper[2] * jnp.eye(covars, dtype=F32)
    sep, sep_border = pl.pallas_call(
        add_kernel,
        out_shape=(shape(m, m), shape(covars, m)),
        in_specs=[smem, vmem, vmem, vmem, vmem],
        out_specs=[vmem] * 2,
        compiler_params=pltpu.CompilerParams(vmem_limit_bytes=32 * 1024 * 1024),
        name="add_right",
    )(meta, own, from_right, border, side_right)
    return (sep[None], fill[None], sep_border[None], tip)


def solution(mesh):
    in_specs = (
        P("groups"),
        P(),
        P("groups"),
        P(None, ("groups", "tm"), None),
        P(None, ("groups", "tm"), None),
        P(None, ("groups", "tm"), None),
    )
    out_specs = (
        P(("groups", "tm"), None, None),
        P(("groups", "tm"), None, None),
        P(("groups", "tm"), None, None),
        P("groups", None),
    )
    return jax.shard_map(local, mesh=mesh, in_specs=in_specs, out_specs=out_specs, check_vma=False)
```

profile of v0, /device:TPU:0, one launch (start us, length us, event | category | flops | bytes accessed | tf_op | source)
XLA Modules:
  0.0 107.6 jit_solution(6809977025313889394)
XLA Ops:
  0.6 0.8 convert_reduce_fusion
  1.4 0.1 convert_element_type.9
  1.5 0.8 reduce.1
  2.3 0.1 concatenate.8
  2.3 1.0 reduce.2
  3.3 0.1 concatenate.9
  3.4 0.0 copy-start.3
  3.5 0.1 copy.11
  3.5 0.8 reshape.23
  4.3 7.4 %all-to-all-start = ((f32[16,1,1536]{2,1,0:T(1,128)}), f32[16,1,1536]{2,1,0:T(1,128)S(1)}, u32[]{:S(2)}, u32[]{:S(2)}) async-start(f32[16,1,1536]{2,1,0:T(1,128)} %reshape.23), calls=%async_computation | async-start | bytes 196608 | tf_op jit(solution)/shard_map/all_to_all | solution.py:327
  11.7 1.4 %fusion = (s32[]{:T(128)}, s32[]{:T(128)}, s32[]{:T(128)}) fusion(s32[16]{0:T(128)} %param.8, s32[]{:T(128)} %axis_index.12, s32[]{:T(128)S(6)} %add.9), kind=kLoop, calls=%fused_computation.7 | loop fusion | flops 141 | bytes 84 | tf_op jit(solution)/shard_map/reduce_sum | solution.py:331
  13.8 2.0 %pad_add_fusion.meta_ref = s32[4]{0:T(128)} fusion(s32[1]{0:T(128)} %bitcast.3, s32[1]{0:T(128)} %bitcast.2, s32[1]{0:T(128)} %bitcast.1, s32[1]{0:T(128)} %bitcast), kind=kLoop, calls=%fused_computation.10 | loop fusion | flops 12 | bytes 32 | tf_op jit(solution)/shard_map/stack | solution.py:334
  15.7 0.0 copy-start.2
  15.7 3.4 %all-to-all-done = f32[16,1,1536]{2,1,0:T(1,128)S(1)} async-done(((f32[16,1,1536]{2,1,0:T(1,128)}), f32[16,1,1536]{2,1,0:T(1,128)S(1)}, u32[]{:S(2)}, u32[]{:S(2)}) %all-to-all-start) | async-done | bytes 98336 | tf_op jit(solution)/shard_map/all_to_all | solution.py:327
  19.1 0.5 broadcast.8
  19.6 0.9 reduce.4
  20.5 0.1 reshape.24
  20.7 0.7 reshape.19.recs_ref
  21.4 36.8 %partition.1 = (f32[768,768]{1,0:T(8,128)}, f32[768,768]{1,0:T(8,128)}, f32[2688,128]{1,0:T(8,128)}, f32[16,768]{1,0:T(8,128)}, f32[16,768]{1,0:T(8,128)}, /*index=5*/f32[16,16]{1,0:T(8,128)}) custom-call(f32[3]{0:T(128)} %hyper_ref.1, s32[4]{0:T(128)} %pad_add_fusion.meta_ref, f32[768,768]{1,0:T(8,128)} %prec_ref.1, f32[24,1024]{1,0:T(8,128)} %reshape.19.recs_ref), custom_call_target="tpu_custom_call" | custom-call | tf_op jit(solution)/shard_map/partition/pallas_call | solution.py:343
  58.2 1.3 %collective-permute-start = (f32[2688,128]{1,0:T(8,128)}, f32[2688,128]{1,0:T(8,128)S(1)}, u32[]{:S(2)}, u32[]{:S(2)}) collective-permute-start(f32[2688,128]{1,0:T(8,128)} %get-tuple-element.13), channel_id=1, source_target_pairs={{1,0},{2,1},{3,2},{4,3},{5,4},{6,5},{7,6},{8,7},{9,8},{10,9},{11,1... | collective-permute-start | bytes 4128776 | tf_op jit(solution)/shard_map/ppermute | solution.py:374
  59.5 0.0 copy-done.3
  59.5 0.6 slice.3
  60.1 1.3 %collective-permute-start.1 = (f32[16,768]{1,0:T(8,128)}, f32[16,768]{1,0:T(8,128)S(1)}, u32[]{:S(2)}, u32[]{:S(2)}) collective-permute-start(f32[16,768]{1,0:T(8,128)} %get-tuple-element.15), channel_id=1, source_target_pairs={{1,0},{2,1},{3,2},{4,3},{5,4},{6,5},{7,6},{8,7},{9,8},{10,9},{11,1... | collective-permute-start | bytes 147464 | tf_op jit(solution)/shard_map/ppermute | solution.py:375
  61.4 40.2 %psum.7 = f32[16,16]{1,0:T(8,128)S(1)} all-reduce(f32[16,16]{1,0:T(8,128)} %get-tuple-element.19), channel_id=1, replica_groups=mesh['groups'=2,'tm'=16] {'tm'}, use_global_device_ids=true, to_apply=%region_3.4 | all-reduce | flops 256 | bytes 2048 | tf_op jit(solution)/shard_map/psum | solution.py:376
  101.6 1.2 %select_add_fusion = f32[16,16]{1,0:T(8,128)} fusion(f32[16,16]{1,0:T(8,128)S(1)} %psum.7, f32[]{:T(128)} %bitcast.9), kind=kLoop, calls=%fused_computation.2 | loop fusion | flops 768 | bytes 2052 | tf_op jit(solution)/shard_map/add | solution.py:376
  102.8 0.0 collective-permute-done.1.side_ref
  102.8 0.0 collective-permute-done.packed_ref
  102.8 0.0 copy-done.2
  102.8 0.0 copy-start
  102.9 1.7 %copy-done = f32[768,768]{1,0:T(8,128)S(1)} copy-done((f32[768,768]{1,0:T(8,128)S(1)}, f32[768,768]{1,0:T(8,128)}, u32[]{:S(2)}) %copy-start) | copy-done | bytes 2359320
  104.5 0.8 copy-done.1
  105.3 2.3 %add_right.1 = (f32[768,768]{1,0:T(8,128)}, f32[16,768]{1,0:T(8,128)}) custom-call(s32[4]{0:T(128)S(1)} %copy-done.2, f32[768,768]{1,0:T(8,128)S(1)} %copy-done, f32[2688,128]{1,0:T(8,128)S(1)} %collective-permute-done.packed_ref, f32[16,768]{1,0:T(8,128)S(1)} %copy-done.1, f32[16,768]{1,0:T(8,128)S(1)} %collective-permute-done.1.side_ref), custom_call_target="tpu_custom_call" | custom-call | tf_op jit(solution)/shard_map/add_right/pallas_call | solution.py:377
  (3 shorter events, 0.1 us)
Async XLA Ops:
  3.4 56.1 %copy-start.3 = (f32[3]{0:T(128)S(1)}, f32[3]{0:T(128)}, u32[]{:S(2)}) copy-start(f32[3]{0:T(128)} %hyper_ref.1) | copy-start | bytes 40
  4.3 14.8 %all-to-all-start = ((f32[16,1,1536]{2,1,0:T(1,128)}), f32[16,1,1536]{2,1,0:T(1,128)S(1)}, u32[]{:S(2)}, u32[]{:S(2)}) async-start(f32[16,1,1536]{2,1,0:T(1,128)} %reshape.23), calls=%async_computation | async-start | bytes 196608 | tf_op jit(solution)/shard_map/all_to_all | solution.py:327
  15.7 87.1 %copy-start.2 = (s32[4]{0:T(128)S(1)}, s32[4]{0:T(128)}, u32[]{:S(2)}) copy-start(s32[4]{0:T(128)} %pad_add_fusion.meta_ref) | copy-start | bytes 52
  58.2 44.6 %collective-permute-start = (f32[2688,128]{1,0:T(8,128)}, f32[2688,128]{1,0:T(8,128)S(1)}, u32[]{:S(2)}, u32[]{:S(2)}) collective-permute-start(f32[2688,128]{1,0:T(8,128)} %get-tuple-element.13), channel_id=1, source_target_pairs={{1,0},{2,1},{3,2},{4,3},{5,4},{6,5},{7,6},{8,7},{9,8},{10,9},{11,1... | collective-permute-start | bytes 4128776 | tf_op jit(solution)/shard_map/ppermute | solution.py:374
  60.1 42.7 %collective-permute-start.1 = (f32[16,768]{1,0:T(8,128)}, f32[16,768]{1,0:T(8,128)S(1)}, u32[]{:S(2)}, u32[]{:S(2)}) collective-permute-start(f32[16,768]{1,0:T(8,128)} %get-tuple-element.15), channel_id=1, source_target_pairs={{1,0},{2,1},{3,2},{4,3},{5,4},{6,5},{7,6},{8,7},{9,8},{10,9},{11,1... | collective-permute-start | bytes 147464 | tf_op jit(solution)/shard_map/ppermute | solution.py:375
  102.8 1.7 %copy-start = (f32[768,768]{1,0:T(8,128)S(1)}, f32[768,768]{1,0:T(8,128)}, u32[]{:S(2)}) copy-start(f32[768,768]{1,0:T(8,128)} %get-tuple-element.12.own_ref) | copy-start | bytes 7077892
  104.5 0.8 copy-start.1
where the time goes:
time: 109 us; the launch traced here: 108 us
  blocking collectives  40.2 us (37%)
  Pallas kernels  39.1 us (36%)
  starting transfers between devices  9.95 us (9%)
  other arithmetic  8.02 us (7%)
  local copies, waits for them, and re-layouts  5.59 us (5%)
  waiting for transfers between devices  3.39 us (3%)
  between operations  1.39 us (1%)
    psum x1, blocking collectives, local(): tip = lax.psum(tip, 'tm') + hyper[2] * jnp.eye(covars, dtype=F32)  40.2 us
    pallas_call x1, Pallas kernels, local(): pl.pallas_call(functools.partial(partition_kernel, chunk, nblk), out_shap...  36.8 us
    all_to_all x1, starting transfers between devices, local(): lax.all_to_all(packed, 'tm', split_axis=0, concat_axis=0, tiled=True)  7.39 us
    all_to_all x1, waiting for transfers between devices, local(): lax.all_to_all(packed, 'tm', split_axis=0, concat_axis=0, tiled=True)  3.38 us
    unnamed x10, local copies, waits for them, and re-layouts  3.36 us
    pallas_call x1, Pallas kernels, local(): pl.pallas_call(add_kernel, out_shape=(shape(m, m), shape(covars, m)), in_...  2.29 us
  transfers between devices with their start and end apart: 3, of which 1 were waited for; matrix products, arithmetic and copies ran while one was open for 5% of the time, Pallas kernels for 0%

commit v1 on v0

--- a/solution.py
+++ b/solution.py
@@ -8,6 +8,7 @@
 from jax.sharding import PartitionSpec as P
 
 HIGHEST = lax.Precision.HIGHEST
+MESH = pl.DeviceIdType.MESH
 BF = jnp.bfloat16
 F32 = jnp.float32
 PAD = 128
@@ -45,31 +46,77 @@
     return 2.0 / (1.0 + q), 2.0 * q / (1.0 + q)
 
 
-def partition_kernel(
-    chunk, nblk, hyper_ref, meta_ref, prec_ref, recs_ref,
-    sep_ref, fill_ref, packed_ref, border_ref, lateral_ref, tip_ref,
-    sh, sl, h1, b1, ah, al, x, res, rth, rtl, yt, rest, wt, a32, x32, t32,
+def greet(tm):
+    me = lax.axis_index("tm")
+    barrier = pltpu.get_barrier_semaphore()
+
+    def signal(i, _):
+        pl.semaphore_signal(
+            barrier, inc=1, device_id={"tm": lax.rem(me + i, tm)}, device_id_type=MESH
+        )
+        return 0
+
+    lax.fori_loop(1, tm, signal, 0)
+    pl.semaphore_wait(barrier, tm - 1)
+    return me
+
+
+def to_all(tm, me, source, slots, send_sem, recv_sem):
+    def start(i, _):
+        to = lax.rem(me + i, tm)
+        pltpu.make_async_remote_copy(
+            src_ref=source(to), dst_ref=slots.at[me], send_sem=send_sem.at[to],
+            recv_sem=recv_sem.at[me], device_id={"tm": to}, device_id_type=MESH,
+        ).start()
+        return 0
+
+    def finish(i, _):
+        to = lax.rem(me + i, tm)
+        copy = pltpu.make_async_remote_copy(
+            src_ref=source(to), dst_ref=slots.at[to], send_sem=send_sem.at[to],
+            recv_sem=recv_sem.at[to], device_id={"tm": to}, device_id_type=MESH,
+        )
+        copy.wait_send()
+        copy.wait_recv()
+        return 0
+
+    lax.fori_loop(1, tm, start, 0)
+    lax.fori_loop(1, tm, finish, 0)
+
+
+def readings_kernel(
+    tm, index_ref, value_ref, cov_ref, out_ref, stage, outgoing, slots, send_sem, recv_sem
 ):
-    m = prec_ref.shape[0]
-    covars = border_ref.shape[0]
-    rho, tau = hyper_ref[0], hyper_ref[1]
-    c_diag = (1.0 + rho * rho) * tau
-    c_off = -rho * tau
-    my_end, length, position = meta_ref[0], meta_ref[1], meta_ref[2]
-    end_f = my_end.astype(F32)
-    two = length == 2
-
-    sep_ref[...] = c_diag * prec_ref[...]
-    h1[...] = c_diag * prec_ref[...]
-    b1[...] = jnp.zeros_like(b1)
-    border_ref[...] = jnp.zeros_like(border_ref)
-    tip_ref[...] = jnp.zeros_like(tip_ref)
+    cap = outgoing.shape[2]
+    stage[0:4, :] = index_ref[:, 0, :].astype(F32)
+    stage[4:8, :] = value_ref[:, 0, :]
+    stage[8:, :] = cov_ref[:, 0, :]
+    for p in range(tm):
+        outgoing[p] = stage[:, p * cap : (p + 1) * cap]
+    me = greet(tm)
+    slots[me] = outgoing[me]
+    to_all(tm, me, lambda p: outgoing.at[p], slots, send_sem, recv_sem)
+    for p in range(tm):
+        out_ref[:, p * cap : (p + 1) * cap] = slots[p]
+
+
+def tip_kernel(tm, hyper_ref, mine_ref, out_ref, slots, send_sem, recv_sem):
+    rows, cols = mine_ref.shape
+    me = greet(tm)
+    slots[me] = mine_ref[...]
+    to_all(tm, me, lambda p: mine_ref, slots, send_sem, recv_sem)
+    total = hyper_ref[2] * eye_part(rows, cols, 0)
+    total = lax.fori_loop(0, tm, lambda p, t: t + slots[p], total)
+    out_ref[...] = total[:, : out_ref.shape[1]]
+
+
+def day_sums(chunk, nblk, wanted, end_f, recs_ref, covars, sh, sl, hess_ref, border_ref, tip_ref):
+    m = hess_ref.shape[0]
 
     def add_chunk(j, _):
         lanes = pl.ds(pl.multiple_of(j * chunk, chunk), chunk)
         slot = end_f - recs_ref[0:1, lanes]
-        m0 = jnp.where(slot == 0.0, 1.0, 0.0)
-        m1 = jnp.where(slot == 1.0, 1.0, 0.0)
+        keep = jnp.where(slot == wanted, 1.0, 0.0).astype(BF)
         root = jnp.exp(0.5 * recs_ref[4:5, lanes])
         ids = [recs_ref[u : u + 1, lanes] for u in (1, 2, 3)]
         vals = [recs_ref[u : u + 1, lanes] * root for u in (5, 6, 7)]
@@ -89,24 +136,59 @@
         z = recs_ref[8 : 8 + covars, lanes] * root
         z = jnp.concatenate([z, jnp.zeros((PAD - covars, chunk), F32)], axis=0)
         zh, zl = split(z)
-        tip_ref[...] += nt3(zh, zl, zh, zl)[:covars, :covars]
-        m0h = m0.astype(BF)
-        m1h = m1.astype(BF)
+        if tip_ref is not None:
+            tip_ref[...] += nt3(zh, zl, zh, zl)[:covars]
 
         def grow(i, _):
             rows = pl.ds(pl.multiple_of(i * nblk, nblk), nblk)
-            bh, bl = sh[rows, :], sl[rows, :]
-            bh0, bl0, bh1, bl1 = bh * m0h, bl * m0h, bh * m1h, bl * m1h
-            sep_ref[:, rows] += nt3(sh[...], sl[...], bh0, bl0)
-            h1[:, rows] += nt3(sh[...], sl[...], bh1, bl1)
-            border_ref[:, rows] += nt3(zh, zl, bh0, bl0)[:covars]
-            b1[:, rows] += nt3(zh, zl, bh1, bl1)
+            bh, bl = sh[rows, :] * keep, sl[rows, :] * keep
+            hess_ref[:, rows] += nt3(sh[...], sl[...], bh, bl)
+            border_ref[:, rows] += nt3(zh, zl, bh, bl)[: border_ref.shape[0]]
             return 0
 
         lax.fori_loop(0, m // nblk, grow, 0)
         return 0
 
     lax.fori_loop(0, recs_ref.shape[1] // chunk, add_chunk, 0)
+
+
+def last_day(lens_ref):
+    me = lax.axis_index("tm")
+    return me, lax.fori_loop(0, me + 1, lambda p, t: t + lens_ref[p], jnp.int32(-1))
+
+
+def separator_kernel(
+    chunk, nblk, hyper_ref, lens_ref, prec_ref, recs_ref, after_ref, sep_ref, border_ref, sh, sl
+):
+    del after_ref
+    rho, tau = hyper_ref[0], hyper_ref[1]
+    _, my_end = last_day(lens_ref)
+    sep_ref[...] = (1.0 + rho * rho) * tau * prec_ref[...]
+    border_ref[...] = jnp.zeros_like(border_ref)
+    covars = border_ref.shape[0]
+    day_sums(
+        chunk, nblk, 0.0, my_end.astype(F32), recs_ref, covars, sh, sl, sep_ref, border_ref, None
+    )
+
+
+def partition_kernel(
+    chunk, nblk, covars, hyper_ref, lens_ref, prec_ref, recs_ref,
+    fill_ref, packed_ref, tip_ref,
+    sh, sl, h1, b1, ah, al, x, res, rth, rtl, yt, rest, wt, a32, x32, t32,
+):
+    m = prec_ref.shape[0]
+    rho, tau = hyper_ref[0], hyper_ref[1]
+    c_diag = (1.0 + rho * rho) * tau
+    c_off = -rho * tau
+    position, my_end = last_day(lens_ref)
+    two = lens_ref[position] == 2
+
+    h1[...] = c_diag * prec_ref[...]
+    b1[...] = jnp.zeros_like(b1)
+    tip_ref[...] = jnp.zeros_like(tip_ref)
+    day_sums(
+        chunk, nblk, 1.0, my_end.astype(F32), recs_ref, covars, sh, sl, h1, b1, tip_ref
+    )
 
     picked = eye_part(m, m, 0) * h1[...]
     d_row = lax.rsqrt(jnp.sum(picked, axis=0, keepdims=True))
@@ -182,16 +264,14 @@
     def put_result(cols_lo, width, col):
         cols = pl.ds(cols_lo, width)
         u = jnp.where(two, -col[:m], 0.0)
-        sep_ref[:, cols] += u
+        h1[:, cols] = u
         fill_ref[:, cols] = jnp.where(
             position == 0, 0.0, jnp.where(two, u, c_off * prec_ref[:, cols])
         )
-        side = jnp.where(two, -col[m : m + covars], 0.0)
-        border_ref[:, cols] += side
-        lateral_ref[:, cols] = side
+        b1[0:covars, cols] = jnp.where(two, -col[m : m + covars], 0.0)
 
     def put_tip(block):
-        tip_ref[...] += jnp.where(two, -block[:covars, :covars], 0.0)
+        tip_ref[...] += jnp.where(two, -block[:covars], 0.0)
 
     @pl.when(good)
     def _():
@@ -291,25 +371,32 @@
     at = 0
     for r in range(m // TILE):
         for c in range(r + 1):
-            packed_ref[at * TILE : (at + 1) * TILE, :] = fill_ref[
+            packed_ref[at * TILE : (at + 1) * TILE, :] = h1[
                 r * TILE : (r + 1) * TILE, c * TILE : (c + 1) * TILE
             ]
             at += 1
-
-
-def add_kernel(meta_ref, own_ref, packed_ref, border_ref, side_ref, sep_ref, out_border_ref):
+    for r in range(m // TILE):
+        lo = at * TILE + r * covars
+        packed_ref[lo : lo + covars, :] = b1[0:covars, r * TILE : (r + 1) * TILE]
+
+
+def add_kernel(own_ref, mine_ref, right_ref, border_ref, sep_ref, out_border_ref):
     m = own_ref.shape[0]
-    take = meta_ref[3] == 2
+    covars = border_ref.shape[0]
     at = 0
     for r in range(m // TILE):
         for c in range(r + 1):
-            block = jnp.where(take, packed_ref[at * TILE : (at + 1) * TILE, :], 0.0)
+            rows = slice(at * TILE, (at + 1) * TILE)
+            block = mine_ref[rows, :] + right_ref[rows, :]
             rs, cs = slice(r * TILE, (r + 1) * TILE), slice(c * TILE, (c + 1) * TILE)
             sep_ref[rs, cs] = own_ref[rs, cs] + block
             if r != c:
                 sep_ref[cs, rs] = own_ref[cs, rs] + block.T
             at += 1
-    out_border_ref[...] = border_ref[...] + jnp.where(take, side_ref[...], 0.0)
+    for r in range(m // TILE):
+        rows = slice(at * TILE + r * covars, at * TILE + (r + 1) * covars)
+        cs = slice(r * TILE, (r + 1) * TILE)
+        out_border_ref[:, cs] = border_ref[:, cs] + (mine_ref[rows, :] + right_ref[rows, :])
 
 
 def local(hyper, spatial_prec, part_lengths, reading_index, reading_value, reading_cov):
@@ -318,36 +405,39 @@
     tm = lax.axis_size("tm")
     reads = reading_index.shape[2]
     cap = reads // tm
-    position = lax.axis_index("tm")
     fields = 8 + covars
-    packed = jnp.concatenate(
-        [reading_index[:, 0].astype(F32), reading_value[:, 0], reading_cov[:, 0]], axis=0
-    )
-    packed = packed.reshape(fields, tm, cap).transpose(1, 0, 2)
-    packed = lax.all_to_all(packed, "tm", split_axis=0, concat_axis=0, tiled=True)
-    recs = packed.transpose(1, 0, 2).reshape(fields, reads)
-
-    upto = jnp.arange(tm, dtype=jnp.int32)
-    my_end = jnp.sum(jnp.where(upto <= position, part_lengths, 0)) - 1
-    my_len = jnp.sum(jnp.where(upto == position, part_lengths, 0))
-    next_len = jnp.sum(jnp.where(upto == position + 1, part_lengths, 0))
-    meta = jnp.stack([my_end, my_len, position, next_len]).astype(jnp.int32)
-
     chunk = min(reads, 1024)
     nblk = 256 if m % 256 == 0 else 128
     tiles = m // TILE
-    packed_rows = tiles * (tiles + 1) // 2 * TILE
+    packed_rows = tiles * (tiles + 1) // 2 * TILE + tiles * covars
     vmem = pl.BlockSpec(memory_space=pltpu.VMEM)
     smem = pl.BlockSpec(memory_space=pltpu.SMEM)
     shape = lambda *s: jax.ShapeDtypeStruct(s, F32)
-    own, fill, lower, border, lateral, tip = pl.pallas_call(
-        functools.partial(partition_kernel, chunk, nblk),
-        out_shape=(
-            shape(m, m), shape(m, m), shape(packed_rows, TILE),
-            shape(covars, m), shape(covars, m), shape(covars, covars),
+    dma = pltpu.SemaphoreType.DMA
+
+    recs = pl.pallas_call(
+        functools.partial(readings_kernel, tm),
+        out_shape=shape(fields, reads),
+        in_specs=[vmem] * 3,
+        out_specs=vmem,
+        scratch_shapes=[
+            pltpu.VMEM((fields, reads), F32),
+            pltpu.VMEM((tm, fields, cap), F32),
+            pltpu.VMEM((tm, fields, cap), F32),
+            dma((tm,)),
+            dma((tm,)),
+        ],
+        compiler_params=pltpu.CompilerParams(
+            collective_id=0, has_side_effects=True, vmem_limit_bytes=32 * 1024 * 1024
         ),
+        name="readings",
+    )(reading_index, reading_value, reading_cov)
+
+    fill, packed, tip = pl.pallas_call(
+        functools.partial(partition_kernel, chunk, nblk, covars),
+        out_shape=(shape(m, m), shape(packed_rows, TILE), shape(covars, PAD)),
         in_specs=[smem, smem, vmem, vmem],
-        out_specs=[vmem] * 6,
+        out_specs=[vmem] * 3,
         scratch_shapes=[
             pltpu.VMEM((m, chunk), BF),
             pltpu.VMEM((m, chunk), BF),
@@ -366,22 +456,42 @@
             pltpu.VMEM((2, m, m), F32),
             pltpu.VMEM((m + PAD, m), F32),
         ],
-        compiler_params=pltpu.CompilerParams(vmem_limit_bytes=60 * 1024 * 1024),
+        compiler_params=pltpu.CompilerParams(vmem_limit_bytes=58 * 1024 * 1024),
         name="partition",
-    )(hyper, meta, spatial_prec, recs)
-
-    back = [(i + 1, i) for i in range(tm - 1)]
-    from_right = lax.ppermute(lower, "tm", back)
-    side_right = lax.ppermute(lateral, "tm", back)
-    tip = lax.psum(tip, "tm") + hyper[2] * jnp.eye(covars, dtype=F32)
+    )(hyper, part_lengths, spatial_prec, recs)
+
+    from_right = lax.ppermute(packed, "tm", [(i + 1, i) for i in range(tm - 1)])
+    own, border = pl.pallas_call(
+        functools.partial(separator_kernel, chunk, nblk),
+        out_shape=(shape(m, m), shape(covars, m)),
+        in_specs=[smem, smem, vmem, vmem, vmem],
+        out_specs=[vmem] * 2,
+        scratch_shapes=[pltpu.VMEM((m, chunk), BF), pltpu.VMEM((m, chunk), BF)],
+        compiler_params=pltpu.CompilerParams(vmem_limit_bytes=40 * 1024 * 1024),
+        cost_estimate=pl.CostEstimate(
+            flops=6 * m * m * reads, bytes_accessed=8 * m * m, transcendentals=0
+        ),
+        name="separator",
+    )(hyper, part_lengths, spatial_prec, recs, tip)
+    tip = pl.pallas_call(
+        functools.partial(tip_kernel, tm),
+        out_shape=shape(covars, covars),
+        in_specs=[smem, vmem],
+        out_specs=vmem,
+        scratch_shapes=[pltpu.VMEM((tm, covars, PAD), F32), dma((tm,)), dma((tm,))],
+        compiler_params=pltpu.CompilerParams(
+            collective_id=1, has_side_effects=True, vmem_limit_bytes=32 * 1024 * 1024
+        ),
+        name="tip_sum",
+    )(hyper, tip)
     sep, sep_border = pl.pallas_call(
         add_kernel,
         out_shape=(shape(m, m), shape(covars, m)),
-        in_specs=[smem, vmem, vmem, vmem, vmem],
+        in_specs=[vmem] * 4,
         out_specs=[vmem] * 2,
         compiler_params=pltpu.CompilerParams(vmem_limit_bytes=32 * 1024 * 1024),
         name="add_right",
-    )(meta, own, from_right, border, side_right)
+    )(own, packed, from_right, border)
     return (sep[None], fill[None], sep_border[None], tip)
 
 

time: 109 us -> 85.4 us (0.78)
  blocking collectives: 40.2 us -> 0 us
  Pallas kernels: 39.1 us -> 77.9 us
  starting transfers between devices: 9.95 us -> 1.28 us
  other arithmetic: 8.02 us -> 0 us
  waiting for transfers between devices: 3.39 us -> 0.01 us
    psum x1 -> x0, blocking collectives: 40.2 us -> none  [local(): tip = lax.psum(tip, 'tm') + hyper[2] * jnp.eye(covars, dtype=F32)]
    pallas_call x1 -> x4, Pallas kernels: 36.8 us -> 76 us  [the longest x1 30.6 us: local(): pl.pallas_call(functools.partial(partition_kernel, chunk, nblk, covars),...]
    all_to_all x1 -> x0, starting transfers between devices: 7.39 us -> none  [local(): lax.all_to_all(packed, 'tm', split_axis=0, concat_axis=0, tiled=True)]
    all_to_all x1 -> x0, waiting for transfers between devices: 3.38 us -> none  [local(): lax.all_to_all(packed, 'tm', split_axis=0, concat_axis=0, tiled=True)]
    another operation x1 -> x0, other arithmetic: 1.95 us -> none  [local(): meta = jnp.stack([my_end, my_len, position, next_len]).astype(jnp.int32)]
    unnamed x2 -> x0, other arithmetic: 1.76 us -> none
    unnamed x10 -> x21, local copies, waits for them, and re-layouts: 3.36 us -> 5.07 us
    reduce_sum x1 -> x0, other arithmetic: 1.41 us -> none  [local(): my_end = jnp.sum(jnp.where(upto <= position, part_lengths, 0)) - 1]
  transfers between devices with their start and end apart: 3 -> 1, of which waited for: 1 -> 0; matrix products, arithmetic and copies ran while one was open for 5% -> 0% of each run, Pallas kernels for 0% -> 41%
where the time goes in v1:
time: 85.4 us; the launch traced here: 85 us
  Pallas kernels  77.9 us (91%)
  local copies, waits for them, and re-layouts  5.07 us (6%)
  starting transfers between devices  1.28 us (1%)
    pallas_call x1, Pallas kernels, local(): pl.pallas_call(functools.partial(partition_kernel, chunk, nblk, covars),...  30.6 us
    pallas_call x1, Pallas kernels, local(): pl.pallas_call(functools.partial(tip_kernel, tm), out_shape=shape(covars,...  27.1 us
    pallas_call x1, Pallas kernels, local(): pl.pallas_call(functools.partial(readings_kernel, tm), out_shape=shape(fi...  10.6 us
    pallas_call x1, Pallas kernels, local(): pl.pallas_call(functools.partial(separator_kernel, chunk, nblk), out_shap...  7.68 us
    unnamed x21, local copies, waits for them, and re-layouts  5.07 us
    pallas_call x1, Pallas kernels, local(): pl.pallas_call(add_kernel, out_shape=(shape(m, m), shape(covars, m)), in_...  1.85 us
  transfers between devices with their start and end apart: 1, of which 0 were waited for; matrix products, arithmetic and copies ran while one was open for 0% of the time, Pallas kernels for 41%

profile of v1, /device:TPU:0, one launch (start us, length us, event | category | flops | bytes accessed | tf_op | source)
XLA Modules:
  0.0 85.0 jit_solution(4997813398246135049)
XLA Ops:
  0.6 0.0 copy-start.4
  0.6 0.8 copy-done.4
  1.5 0.0 copy-start.5
  1.5 0.7 copy-done.5
  2.2 0.0 copy-start.6
  2.2 0.7 copy-done.6
  2.9 0.0 copy-start.8
  2.9 0.0 copy-start
  2.9 0.0 copy-start.9
  2.9 10.6 %readings.1.recs_ref = f32[24,1024]{1,0:T(8,128)S(1)} custom-call(s32[4,1,1024]{2,1,0:T(1,128)S(1)} %copy-done.5, f32[4,1,1024]{2,1,0:T(1,128)S(1)} %copy-done.6, f32[16,1,1024]{2,1,0:T(1,128)S(1)} %copy-done.4), custom_call_target="tpu_custom_call" | custom-call | tf_op jit(solution)/shard_map/readings/pallas_call | solution.py:418
  13.5 0.0 copy-start.2
  13.6 0.6 copy-done.2
  14.2 30.6 %partition.1 = (f32[768,768]{1,0:T(8,128)}, f32[2784,128]{1,0:T(8,128)}, f32[16,128]{1,0:T(8,128)}) custom-call(f32[3]{0:T(128)} %hyper_ref.5, s32[16]{0:T(128)} %lens_ref.3, f32[768,768]{1,0:T(8,128)} %prec_ref.3, f32[24,1024]{1,0:T(8,128)} %copy-done.2), custom_call_target="tpu_custom_call" | custom-call | tf_op jit(solution)/shard_map/partition/pallas_call | solution.py:436
  44.8 1.3 %collective-permute-start = (f32[2784,128]{1,0:T(8,128)}, f32[2784,128]{1,0:T(8,128)S(1)}, u32[]{:S(2)}, u32[]{:S(2)}) collective-permute-start(f32[2784,128]{1,0:T(8,128)} %get-tuple-element.13.mine_ref), channel_id=1, source_target_pairs={{1,0},{2,1},{3,2},{4,3},{5,4},{6,5},{7,6},{8,7},{9,8},{10,9},{11,1... | collective-permute-start | bytes 4276232 | tf_op jit(solution)/shard_map/ppermute | solution.py:463
  46.1 0.0 copy-done.8
  46.1 0.0 copy-start.7
  46.1 0.7 copy-done.7
  46.8 27.1 %tip_sum.1 = f32[16,16]{1,0:T(8,128)S(1)} custom-call(f32[3]{0:T(128)S(1)} %copy-done.8, f32[16,128]{1,0:T(8,128)S(1)} %copy-done.7), custom_call_target="tpu_custom_call" | custom-call | tf_op jit(solution)/shard_map/tip_sum/pallas_call | solution.py:476
  73.9 0.0 copy-done
  73.9 0.0 copy-done.9
  73.9 0.0 copy-start.3
  73.9 0.9 %copy-done.3 = f32[24,1024]{1,0:T(8,128)S(1)} copy-done((f32[24,1024]{1,0:T(8,128)S(1)}, f32[24,1024]{1,0:T(8,128)}, u32[]{:S(2)}) %copy-start.3) | copy-done | bytes 98328
  74.8 0.0 copy-start.1
  74.8 7.7 %separator.1 = (f32[768,768]{1,0:T(8,128)S(1)}, f32[16,768]{1,0:T(8,128)S(1)}) custom-call(f32[3]{0:T(128)S(1)} %copy-done.8, s32[16]{0:T(128)S(1)} %copy-done.9, f32[768,768]{1,0:T(8,128)S(1)} %copy-done, f32[24,1024]{1,0:T(8,128)S(1)} %copy-done.3, f32[16,128]{1,0:T(8,128)S(1)} %copy-done.7), custom_call_target="tpu_custom_call" | custom-call | flops 3623878656 | bytes 4718592 | tf_op jit(solution)/shard_map/separator/pallas_call | solution.py:464
  82.5 0.0 collective-permute-done.right_ref
  82.5 0.0 copy-done.1
  82.5 1.8 %add_right.1 = (f32[768,768]{1,0:T(8,128)}, f32[16,768]{1,0:T(8,128)}) custom-call(f32[768,768]{1,0:T(8,128)S(1)} %get-tuple-element.12.own_ref, f32[2784,128]{1,0:T(8,128)S(1)} %copy-done.1, f32[2784,128]{1,0:T(8,128)S(1)} %collective-permute-done.right_ref, f32[16,768]{1,0:T(8,128)S(1)} %get-tuple-element.14.border_ref), custom_call_target="tpu_custom_call" | custom-call | tf_op jit(solution)/shard_map/add_right/pallas_call | solution.py:487
  84.4 0.6 copy.11
Async XLA Ops:
  0.6 0.8 copy-start.4
  1.5 0.7 copy-start.5
  2.2 0.7 copy-start.6
  2.9 43.2 %copy-start.8 = (f32[3]{0:T(128)S(1)}, f32[3]{0:T(128)}, u32[]{:S(2)}) copy-start(f32[3]{0:T(128)} %hyper_ref.5) | copy-start | bytes 40
  2.9 71.0 %copy-start = (f32[768,768]{1,0:T(8,128)S(1)}, f32[768,768]{1,0:T(8,128)}, u32[]{:S(2)}) copy-start(f32[768,768]{1,0:T(8,128)} %prec_ref.3) | copy-start | bytes 7077892
  2.9 71.0 %copy-start.9 = (s32[16]{0:T(128)S(1)}, s32[16]{0:T(128)}, u32[]{:S(2)}) copy-start(s32[16]{0:T(128)} %lens_ref.3) | copy-start | bytes 196
  13.5 0.6 copy-start.2
  44.8 37.7 %collective-permute-start = (f32[2784,128]{1,0:T(8,128)}, f32[2784,128]{1,0:T(8,128)S(1)}, u32[]{:S(2)}, u32[]{:S(2)}) collective-permute-start(f32[2784,128]{1,0:T(8,128)} %get-tuple-element.13.mine_ref), channel_id=1, source_target_pairs={{1,0},{2,1},{3,2},{4,3},{5,4},{6,5},{7,6},{8,7},{9,8},{10,9},{11,1... | collective-permute-start | bytes 4276232 | tf_op jit(solution)/shard_map/ppermute | solution.py:463
  46.1 0.7 copy-start.7
  73.9 0.9 %copy-start.3 = (f32[24,1024]{1,0:T(8,128)S(1)}, f32[24,1024]{1,0:T(8,128)}, u32[]{:S(2)}) copy-start(f32[24,1024]{1,0:T(8,128)} %copy-done.2) | copy-start | bytes 294916
  74.8 7.7 %copy-start.1 = (f32[2784,128]{1,0:T(8,128)S(1)}, f32[2784,128]{1,0:T(8,128)}, u32[]{:S(2)}) copy-start(f32[2784,128]{1,0:T(8,128)} %get-tuple-element.13.mine_ref) | copy-start | bytes 4276228

commit v2 on v1

--- a/solution.py
+++ b/solution.py
@@ -100,7 +100,8 @@
         out_ref[:, p * cap : (p + 1) * cap] = slots[p]
 
 
-def tip_kernel(tm, hyper_ref, mine_ref, out_ref, slots, send_sem, recv_sem):
+def tip_kernel(tm, hyper_ref, mine_ref, after_ref, out_ref, slots, send_sem, recv_sem):
+    del after_ref
     rows, cols = mine_ref.shape
     me = greet(tm)
     slots[me] = mine_ref[...]
@@ -136,14 +137,17 @@
         z = recs_ref[8 : 8 + covars, lanes] * root
         z = jnp.concatenate([z, jnp.zeros((PAD - covars, chunk), F32)], axis=0)
         zh, zl = split(z)
+        sh[m : m + PAD, :] = zh
+        sl[m : m + PAD, :] = zl
         if tip_ref is not None:
             tip_ref[...] += nt3(zh, zl, zh, zl)[:covars]
 
         def grow(i, _):
             rows = pl.ds(pl.multiple_of(i * nblk, nblk), nblk)
             bh, bl = sh[rows, :] * keep, sl[rows, :] * keep
-            hess_ref[:, rows] += nt3(sh[...], sl[...], bh, bl)
-            border_ref[:, rows] += nt3(zh, zl, bh, bl)[: border_ref.shape[0]]
+            both = nt3(sh[...], sl[...], bh, bl)
+            hess_ref[:, rows] += both[:m]
+            border_ref[:, rows] += both[m : m + border_ref.shape[0]]
             return 0
 
         lax.fori_loop(0, m // nblk, grow, 0)
@@ -412,6 +416,7 @@
     packed_rows = tiles * (tiles + 1) // 2 * TILE + tiles * covars
     vmem = pl.BlockSpec(memory_space=pltpu.VMEM)
     smem = pl.BlockSpec(memory_space=pltpu.SMEM)
+    anywhere = pl.BlockSpec(memory_space=pl.ANY)
     shape = lambda *s: jax.ShapeDtypeStruct(s, F32)
     dma = pltpu.SemaphoreType.DMA
 
@@ -439,8 +444,8 @@
         in_specs=[smem, smem, vmem, vmem],
         out_specs=[vmem] * 3,
         scratch_shapes=[
-            pltpu.VMEM((m, chunk), BF),
-            pltpu.VMEM((m, chunk), BF),
+            pltpu.VMEM((m + PAD, chunk), BF),
+            pltpu.VMEM((m + PAD, chunk), BF),
             pltpu.VMEM((m, m), F32),
             pltpu.VMEM((PAD, m), F32),
             pltpu.VMEM((m, m), BF),
@@ -464,9 +469,9 @@
     own, border = pl.pallas_call(
         functools.partial(separator_kernel, chunk, nblk),
         out_shape=(shape(m, m), shape(covars, m)),
-        in_specs=[smem, smem, vmem, vmem, vmem],
+        in_specs=[smem, smem, vmem, vmem, anywhere],
         out_specs=[vmem] * 2,
-        scratch_shapes=[pltpu.VMEM((m, chunk), BF), pltpu.VMEM((m, chunk), BF)],
+        scratch_shapes=[pltpu.VMEM((m + PAD, chunk), BF)] * 2,
         compiler_params=pltpu.CompilerParams(vmem_limit_bytes=40 * 1024 * 1024),
         cost_estimate=pl.CostEstimate(
             flops=6 * m * m * reads, bytes_accessed=8 * m * m, transcendentals=0
@@ -476,14 +481,14 @@
     tip = pl.pallas_call(
         functools.partial(tip_kernel, tm),
         out_shape=shape(covars, covars),
-        in_specs=[smem, vmem],
+        in_specs=[smem, vmem, anywhere],
         out_specs=vmem,
         scratch_shapes=[pltpu.VMEM((tm, covars, PAD), F32), dma((tm,)), dma((tm,))],
         compiler_params=pltpu.CompilerParams(
             collective_id=1, has_side_effects=True, vmem_limit_bytes=32 * 1024 * 1024
         ),
         name="tip_sum",
-    )(hyper, tip)
+    )(hyper, tip, border)
     sep, sep_border = pl.pallas_call(
         add_kernel,
         out_shape=(shape(m, m), shape(covars, m)),

time: 85.4 us -> 75.6 us (0.89)
  Pallas kernels: 77.9 us -> 68.5 us
    pallas_call x1, Pallas kernels: 27.1 us -> 19.2 us  [local(): pl.pallas_call(functools.partial(tip_kernel, tm), out_shape=shape(covars,...]
    unnamed x21 -> x23, local copies, waits for them, and re-layouts: 5.07 us -> 5.09 us
  transfers between devices with their start and end apart: 1 -> 1, of which waited for: 0 -> 0; matrix products, arithmetic and copies ran while one was open for 0% -> 0% of each run, Pallas kernels for 41% -> 35%
where the time goes in v2:
time: 75.6 us
  Pallas kernels  68.5 us (91%)
  local copies, waits for them, and re-layouts  5.09 us (7%)
  starting transfers between devices  1.28 us (2%)
    pallas_call x1, Pallas kernels, local(): pl.pallas_call(functools.partial(partition_kernel, chunk, nblk, covars),...  29.9 us
    pallas_call x1, Pallas kernels, local(): pl.pallas_call(functools.partial(tip_kernel, tm), out_shape=shape(covars,...  19.2 us
    pallas_call x1, Pallas kernels, local(): pl.pallas_call(functools.partial(readings_kernel, tm), out_shape=shape(fi...  10.6 us
    pallas_call x1, Pallas kernels, local(): pl.pallas_call(functools.partial(separator_kernel, chunk, nblk), out_shap...  6.97 us
    unnamed x23, local copies, waits for them, and re-layouts  5.09 us
    pallas_call x1, Pallas kernels, local(): pl.pallas_call(add_kernel, out_shape=(shape(m, m), shape(covars, m)), in_...  1.85 us
  transfers between devices with their start and end apart: 1, of which 0 were waited for; matrix products, arithmetic and copies ran while one was open for 0% of the time, Pallas kernels for 35%

profile of v2, /device:TPU:0, one launch (start us, length us, event | category | flops | bytes accessed | tf_op | source)
XLA Modules:
  0.0 75.6 jit_solution(17912919601385164602)
XLA Ops:
  0.6 0.0 copy-start.4
  0.6 0.8 %copy-done.4 = f32[16,1,1024]{2,1,0:T(1,128)S(1)} copy-done((f32[16,1,1024]{2,1,0:T(1,128)S(1)}, f32[16,1,1024]{2,1,0:T(1,128)}, u32[]{:S(2)}) %copy-start.4) | copy-done | bytes 65560
  1.5 0.0 copy-start.5
  1.5 0.7 copy-done.5
  2.2 0.0 copy-start.6
  2.2 0.7 copy-done.6
  2.9 0.0 copy-start
  2.9 0.0 copy-start.9
  2.9 0.0 copy-start.10
  2.9 10.6 %readings.1.recs_ref = f32[24,1024]{1,0:T(8,128)S(1)} custom-call(s32[4,1,1024]{2,1,0:T(1,128)S(1)} %copy-done.5, f32[4,1,1024]{2,1,0:T(1,128)S(1)} %copy-done.6, f32[16,1,1024]{2,1,0:T(1,128)S(1)} %copy-done.4), custom_call_target="tpu_custom_call" | custom-call | tf_op jit(solution)/shard_map/readings/pallas_call | solution.py:423
  13.5 0.0 copy-start.2
  13.6 0.6 copy-done.2
  14.2 29.9 %partition.1 = (f32[768,768]{1,0:T(8,128)}, f32[2784,128]{1,0:T(8,128)}, f32[16,128]{1,0:T(8,128)}) custom-call(f32[3]{0:T(128)} %hyper_ref.5, s32[16]{0:T(128)} %lens_ref.3, f32[768,768]{1,0:T(8,128)} %prec_ref.3, f32[24,1024]{1,0:T(8,128)} %copy-done.2), custom_call_target="tpu_custom_call" | custom-call | tf_op jit(solution)/shard_map/partition/pallas_call | solution.py:441
  44.1 1.3 %collective-permute-start = (f32[2784,128]{1,0:T(8,128)}, f32[2784,128]{1,0:T(8,128)S(1)}, u32[]{:S(2)}, u32[]{:S(2)}) collective-permute-start(f32[2784,128]{1,0:T(8,128)} %get-tuple-element.13.mine_ref), channel_id=1, source_target_pairs={{1,0},{2,1},{3,2},{4,3},{5,4},{6,5},{7,6},{8,7},{9,8},{10,9},{11,1... | collective-permute-start | bytes 4276232 | tf_op jit(solution)/shard_map/ppermute | solution.py:468
  45.4 0.0 copy-done
  45.4 0.0 copy-done.9
  45.4 0.0 copy-done.10
  45.4 0.0 copy-start.3
  45.4 0.9 %copy-done.3 = f32[24,1024]{1,0:T(8,128)S(1)} copy-done((f32[24,1024]{1,0:T(8,128)S(1)}, f32[24,1024]{1,0:T(8,128)}, u32[]{:S(2)}) %copy-start.3) | copy-done | bytes 98328
  46.3 0.0 copy-start.7
  46.3 0.7 copy-done.7
  47.0 0.0 copy-start.8
  47.0 0.0 copy-start.1
  47.0 7.0 %separator.1 = (f32[768,768]{1,0:T(8,128)S(1)}, f32[16,768]{1,0:T(8,128)S(1)}) custom-call(f32[3]{0:T(128)S(1)} %copy-done.9, s32[16]{0:T(128)S(1)} %copy-done.10, f32[768,768]{1,0:T(8,128)S(1)} %copy-done, f32[24,1024]{1,0:T(8,128)S(1)} %copy-done.3, f32[16,128]{1,0:T(8,128)S(1)} %copy-done.7), custom_call_target="tpu_custom_call" | custom-call | flops 3623878656 | bytes 4718592 | tf_op jit(solution)/shard_map/separator/pallas_call | solution.py:469
  54.0 0.0 copy-done.8
  54.0 19.2 %tip_sum.1 = f32[16,16]{1,0:T(8,128)S(1)} custom-call(f32[3]{0:T(128)S(1)} %copy-done.9, f32[16,128]{1,0:T(8,128)S(1)} %copy-done.8, f32[16,768]{1,0:T(8,128)S(1)} %get-tuple-element.14.border_ref.after_ref), custom_call_target="tpu_custom_call" | custom-call | tf_op jit(solution)/shard_map/tip_sum/pallas_call | solution.py:481
  73.2 0.0 collective-permute-done.right_ref
  73.2 0.0 copy-done.1
  73.2 1.8 %add_right.1 = (f32[768,768]{1,0:T(8,128)}, f32[16,768]{1,0:T(8,128)}) custom-call(f32[768,768]{1,0:T(8,128)S(1)} %get-tuple-element.12.own_ref, f32[2784,128]{1,0:T(8,128)S(1)} %copy-done.1, f32[2784,128]{1,0:T(8,128)S(1)} %collective-permute-done.right_ref, f32[16,768]{1,0:T(8,128)S(1)} %get-tuple-element.14.border_ref.after_ref), custom_call_target="tpu_custom_call" | custom-call | tf_op jit(solution)/shard_map/add_right/pallas_call | solution.py:492
  75.0 0.6 copy.11
Async XLA Ops:
  0.6 0.8 %copy-start.4 = (f32[16,1,1024]{2,1,0:T(1,128)S(1)}, f32[16,1,1024]{2,1,0:T(1,128)}, u32[]{:S(2)}) copy-start(f32[16,1,1024]{2,1,0:T(1,128)} %cov_ref.1) | copy-start | bytes 196612
  1.5 0.7 copy-start.5
  2.2 0.7 copy-start.6
  2.9 42.5 %copy-start = (f32[768,768]{1,0:T(8,128)S(1)}, f32[768,768]{1,0:T(8,128)}, u32[]{:S(2)}) copy-start(f32[768,768]{1,0:T(8,128)} %prec_ref.3) | copy-start | bytes 7077892
  2.9 42.5 %copy-start.9 = (f32[3]{0:T(128)S(1)}, f32[3]{0:T(128)}, u32[]{:S(2)}) copy-start(f32[3]{0:T(128)} %hyper_ref.5) | copy-start | bytes 40
  2.9 42.5 %copy-start.10 = (s32[16]{0:T(128)S(1)}, s32[16]{0:T(128)}, u32[]{:S(2)}) copy-start(s32[16]{0:T(128)} %lens_ref.3) | copy-start | bytes 196
  13.5 0.6 copy-start.2
  44.1 29.1 %collective-permute-start = (f32[2784,128]{1,0:T(8,128)}, f32[2784,128]{1,0:T(8,128)S(1)}, u32[]{:S(2)}, u32[]{:S(2)}) collective-permute-start(f32[2784,128]{1,0:T(8,128)} %get-tuple-element.13.mine_ref), channel_id=1, source_target_pairs={{1,0},{2,1},{3,2},{4,3},{5,4},{6,5},{7,6},{8,7},{9,8},{10,9},{11,1... | collective-permute-start | bytes 4276232 | tf_op jit(solution)/shard_map/ppermute | solution.py:468
  45.4 0.9 %copy-start.3 = (f32[24,1024]{1,0:T(8,128)S(1)}, f32[24,1024]{1,0:T(8,128)}, u32[]{:S(2)}) copy-start(f32[24,1024]{1,0:T(8,128)} %copy-done.2) | copy-start | bytes 294916
  46.3 0.7 copy-start.7
  47.0 7.0 %copy-start.8 = (f32[16,128]{1,0:T(8,128)S(1)}, f32[16,128]{1,0:T(8,128)}, u32[]{:S(2)}) copy-start(f32[16,128]{1,0:T(8,128)} %get-tuple-element.11.after_ref.mine_ref) | copy-start | bytes 24580
  47.0 26.2 %copy-start.1 = (f32[2784,128]{1,0:T(8,128)S(1)}, f32[2784,128]{1,0:T(8,128)}, u32[]{:S(2)}) copy-start(f32[2784,128]{1,0:T(8,128)} %get-tuple-element.13.mine_ref) | copy-start | bytes 4276228
